TPU v7x, 512 devices: a whole 4x8x8 slice. The times are simulated.
512 devices in a mesh: fsdp: 8 (over y_lo, x), seq: 64 (over z, y_hi, core).
Axes of the slice: x: 4, y: 8 (y_hi: 4, y_lo: 2; y = y_hi * 2 + y_lo), z: 8, core: 2. Of those that a mesh axis runs over, the one named last changes fastest.
Arguments:
- q_heads: bfloat16 [8192, 5120], P('seq', 'fsdp'), may hold values from -5 to 5
- k_heads: bfloat16 [8192, 5120], P('seq', 'fsdp'), may hold values from -5 to 5
- v_heads: bfloat16 [8192, 5120], P('seq', 'fsdp'), may hold values from -16 to 16
- out_weight: bfloat16 [5120, 5120], P('fsdp', 'seq'), may hold values from -0.078125 to 0.078125
- out_gate: float32 [5120], P('fsdp'), may hold values from 2 to 20
- tile_map: int32 [64], replicated, may hold values from 0 to 63, as said below
- key_tiles: int32 [64, 4], replicated, may hold values from 0 to 63, as said below
- key_count: int32 [64], replicated, may hold values from 1 to 4, as said below
Outputs:
- attn_out: bfloat16 [5120, 8192], P('fsdp', 'seq')
Inputs may be any that keep to these rules, and one draw needn't show every extreme that they name: `tile_map`: slots 2 * p to 2 * (p + 1) - 1 hold the tiles 2 * p to 2 * (p + 1) - 1 in some order; every tile is held once. `key_tiles`: row t starts with t itself; its entries are distinct tiles u with |u // 2 - t // 2| <= 1; only the first key_count[t] entries are used. `key_count`: some tile uses all 4 entries.
All inputs are finite; a program needn't handle non-finite values.
Results may differ from a plain program's by a relative error of at most 0.02.
Values may be sent and summed in bfloat16 or wider, within the bound.
A program may use at most 64 MiB of HBM per device.

v0:
```python
import jax
import jax.numpy as jnp
from jax import lax
from jax.sharding import PartitionSpec as P

HD = 128
TILE = 128


neg_large = -1e30


def shifted(block, axis, distance):
    devices = range(lax.axis_size(axis))
    route = [(i - distance, i) for i in devices if i - distance in devices]
    return lax.ppermute(block, axis, route)


def on_device(q_heads, k_heads, v_heads, out_weight, out_gate, tile_map, key_tiles, key_count):
    tok_rows = q_heads.shape[0]
    tiles_here = tok_rows // TILE
    head_count = q_heads.shape[1] // HD
    seq_size = lax.axis_size("seq")
    reach_devices = 2 * seq_size // (seq_size // 2) - 1
    my_index = lax.axis_index("seq")
    score_scale = 1.0 / float(HD) ** 0.5
    slot_total = seq_size * tiles_here
    weight_full = lax.all_gather(out_weight, "seq", axis=1, tiled=True)
    query_rows = q_heads.reshape(tok_rows, head_count, HD)
    local_slots = jnp.arange(tiles_here, dtype=jnp.int32)
    my_slots = my_index * tiles_here + local_slots
    my_tiles = jnp.take(tile_map, my_slots)
    key_lists = jnp.take(key_tiles, my_tiles, axis=0)
    list_lengths = jnp.take(key_count, my_tiles)
    list_valid = jnp.arange(key_lists.shape[1], dtype=jnp.int32)[None, :] < list_lengths[:, None]

    def absorb(state_now, key_value, key_slots):
        inside = (key_slots >= 0) & (key_slots < slot_total)
        safe_slots = jnp.clip(key_slots, 0, slot_total - 1)
        key_ids = jnp.take(tile_map, safe_slots)
        block_tiles = key_slots.shape[0]
        matches = (key_lists[:, :, None] == key_ids[None, None, :]) & list_valid[:, :, None]
        allowed = jnp.any(matches, axis=1) & inside[None, :]
        running, denominator, numerator = state_now
        token_mask = jnp.broadcast_to(
            allowed[:, None, :, None], (tiles_here, TILE, block_tiles, TILE)
        )
        token_mask = token_mask.reshape(tok_rows, block_tiles * TILE)
        key_block = key_value[0].reshape(block_tiles * TILE, head_count, HD)
        value_block = key_value[1].reshape(block_tiles * TILE, head_count, HD)
        scores = (
            jnp.einsum("qhd,khd->hqk", query_rows, key_block, preferred_element_type=jnp.float32)
            * score_scale
        )
        masked = jnp.where(token_mask[None], scores, neg_large)
        newest = jnp.maximum(running, jnp.max(masked, axis=2))
        factor = jnp.exp(running - newest)
        weights = jnp.where(token_mask[None], jnp.exp(masked - newest[:, :, None]), 0.0)
        denominator = denominator * factor + jnp.sum(weights, axis=2)
        numerator = numerator * factor[:, :, None] + jnp.einsum(
            "hqk,khd->hqd",
            weights.astype(jnp.bfloat16),
            value_block,
            preferred_element_type=jnp.float32,
        )
        return (newest, denominator, numerator)

    start_state = (
        jnp.full((head_count, tok_rows), neg_large, jnp.float32),
        jnp.zeros((head_count, tok_rows), jnp.float32),
        jnp.zeros((head_count, tok_rows, HD), jnp.float32),
    )
    own_pair = jnp.stack((k_heads, v_heads))
    state_now = absorb(start_state, own_pair, my_slots)

    def turn(turn_index, loop_state):
        state_inner, lower_pair, upper_pair = loop_state
        lower_pair = shifted(lower_pair, "seq", 1)
        upper_pair = shifted(upper_pair, "seq", -1)
        lower_slots = (my_index - turn_index - 1) * tiles_here + local_slots
        upper_slots = (my_index + turn_index + 1) * tiles_here + local_slots
        both_pairs = jnp.concatenate((lower_pair, upper_pair), axis=1)
        both_slots = jnp.concatenate((lower_slots, upper_slots))
        return (absorb(state_inner, both_pairs, both_slots), lower_pair, upper_pair)

    state_now = lax.fori_loop(0, reach_devices, turn, (state_now, own_pair, own_pair))[0]
    running, denominator, numerator = state_now
    attention = numerator / denominator[:, :, None]
    attention = (
        jnp.transpose(attention, (1, 0, 2)).reshape(tok_rows, head_count * HD).astype(jnp.bfloat16)
    )
    summed = lax.psum_scatter(
        lax.dot_general(
            weight_full, attention, (((0,), (1,)), ((), ())), preferred_element_type=jnp.float32
        ).astype(jnp.bfloat16),
        "fsdp",
        scatter_dimension=0,
        tiled=True,
    ).astype(jnp.float32)
    return (out_gate[:, None] * summed).astype(jnp.bfloat16)


def solution(mesh):
    return jax.shard_map(
        on_device,
        mesh=mesh,
        in_specs=(
            P("seq", "fsdp"),
            P("seq", "fsdp"),
            P("seq", "fsdp"),
            P("fsdp", "seq"),
            P("fsdp"),
            P(),
            P(),
            P(),
        ),
        out_specs=P("fsdp", "seq"),
        check_vma=False,
    )
```

profile of v0, /device:TPU:16, one launch (start us, length us, event | category | flops | bytes accessed | tf_op | source)
XLA Modules:
  0.0 171.6 jit_solution(1821833271711516416)
XLA Ops:
  6.5 0.7 all-gather.2.cloned.1.call-update
  7.3 1.4 fusion.24
  9.3 1.3 dynamic-slice.12
  10.7 0.1 copy.72
  10.8 1.1 copy.51
  11.9 1.1 copy.52
  12.9 1.1 copy.55
  14.1 0.2 copy.60
  15.5 0.7 and_reduce_fusion.1
  16.9 0.3 fusion.25
  17.2 0.3 convolution_add_fusion.1
  17.5 48.9 %while.28 = (s32[]{:T(128)}, f32[5,128]{1,0:T(8,128)S(1)}, f32[5,128]{1,0:T(8,128)S(1)}, f32[5,128,128]{2,1,0:T(8,128)S(1)}, bf16[2,128,640]{1,2,0:T(8,128)(2,1)...) while((s32[]{:T(128)}, f32[5,128]{1,0:T(8,128)S(1)}, ...), condition=%wide.region_7.8_spmd.clone, body=%wide.region_3.7_spmd.clone.sunk | while | flops 85526848 | bytes 10040697 | solution.py:86
  17.5 1.9 %collective-permute-start = (bf16[2,128,640]{1,2,0:T(8,128)(2,1)S(1)}, bf16[2,128,640]{1,2,0:T(8,128)(2,1)S(1)}, u32[]{:S(2)}, u32[]{:S(2)}) collective-permute-start(bf16[2,128,640]{1,2,0:T(8,128)(2,1)S(1)} %get-tuple-element.506), channel_id=1, source_target_pairs={{0,1},{1,2},{2,3},{3,4},{4,5},{5,6},{6,7},{7,8},{8,9},{9,10},{10,1... | collective-permute-start | bytes 983048 | tf_op jit(solution)/shard_map/while/body/eval_jaxpr/ppermute | solution.py:16
  19.5 4.5 %collective-permute-start.1 = (bf16[2,128,640]{1,2,0:T(8,128)(2,1)S(1)}, bf16[2,128,640]{1,2,0:T(8,128)(2,1)S(1)}, u32[]{:S(2)}, u32[]{:S(2)}) collective-permute-start(bf16[2,128,640]{1,2,0:T(8,128)(2,1)S(1)} %get-tuple-element.507), channel_id=1, source_target_pairs={{1,0},{2,1},{3,2},{4,3},{5,4},{6,5},{7,6},{8,7},{9,8},{10,9},{11,1... | collective-permute-start | bytes 983048 | tf_op jit(solution)/shard_map/while/body/eval_jaxpr/ppermute | solution.py:16
  24.1 1.3 gather_fusion
  25.4 0.1 and_select_fusion.2
  25.5 0.1 and_reduce_fusion.3
  25.8 2.0 %collective-permute-done = bf16[2,128,640]{1,2,0:T(8,128)(2,1)S(1)} collective-permute-done((bf16[2,128,640]{1,2,0:T(8,128)(2,1)S(1)}, bf16[2,128,640]{1,2,0:T(8,128)(2,1)S(1)}, u32[]{:S(2)}, u32[]{:S(2)}) %collective-permute-start) | collective-permute-done | bytes 327712 | tf_op jit(solution)/shard_map/while/body/eval_jaxpr/ppermute | solution.py:16
  27.8 5.2 %collective-permute-done.1 = bf16[2,128,640]{1,2,0:T(8,128)(2,1)S(1)} collective-permute-done((bf16[2,128,640]{1,2,0:T(8,128)(2,1)S(1)}, bf16[2,128,640]{1,2,0:T(8,128)(2,1)S(1)}, u32[]{:S(2)}, u32[]{:S(2)}) %collective-permute-start.1) | collective-permute-done | bytes 327712 | tf_op jit(solution)/shard_map/while/body/eval_jaxpr/ppermute | solution.py:16
  33.2 0.3 fusion.48
  33.5 0.1 fusion.49
  33.7 0.5 convolution_add_fusion.3
  34.2 6.5 %collective-permute-start = (bf16[2,128,640]{1,2,0:T(8,128)(2,1)S(1)}, bf16[2,128,640]{1,2,0:T(8,128)(2,1)S(1)}, u32[]{:S(2)}, u32[]{:S(2)}) collective-permute-start(bf16[2,128,640]{1,2,0:T(8,128)(2,1)S(1)} %get-tuple-element.506), channel_id=1, source_target_pairs={{0,1},{1,2},{2,3},{3,4},{4,5},{5,6},{6,7},{7,8},{8,9},{9,10},{10,1... | collective-permute-start | bytes 983048 | tf_op jit(solution)/shard_map/while/body/eval_jaxpr/ppermute | solution.py:16
  40.7 1.9 %collective-permute-start.1 = (bf16[2,128,640]{1,2,0:T(8,128)(2,1)S(1)}, bf16[2,128,640]{1,2,0:T(8,128)(2,1)S(1)}, u32[]{:S(2)}, u32[]{:S(2)}) collective-permute-start(bf16[2,128,640]{1,2,0:T(8,128)(2,1)S(1)} %get-tuple-element.507), channel_id=1, source_target_pairs={{1,0},{2,1},{3,2},{4,3},{5,4},{6,5},{7,6},{8,7},{9,8},{10,9},{11,1... | collective-permute-start | bytes 983048 | tf_op jit(solution)/shard_map/while/body/eval_jaxpr/ppermute | solution.py:16
  42.7 1.3 gather_fusion
  44.0 0.1 and_select_fusion.2
  44.1 0.1 and_reduce_fusion.3
  44.4 2.0 %collective-permute-done = bf16[2,128,640]{1,2,0:T(8,128)(2,1)S(1)} collective-permute-done((bf16[2,128,640]{1,2,0:T(8,128)(2,1)S(1)}, bf16[2,128,640]{1,2,0:T(8,128)(2,1)S(1)}, u32[]{:S(2)}, u32[]{:S(2)}) %collective-permute-start) | collective-permute-done | bytes 327712 | tf_op jit(solution)/shard_map/while/body/eval_jaxpr/ppermute | solution.py:16
  46.4 5.3 %collective-permute-done.1 = bf16[2,128,640]{1,2,0:T(8,128)(2,1)S(1)} collective-permute-done((bf16[2,128,640]{1,2,0:T(8,128)(2,1)S(1)}, bf16[2,128,640]{1,2,0:T(8,128)(2,1)S(1)}, u32[]{:S(2)}, u32[]{:S(2)}) %collective-permute-start.1) | collective-permute-done | bytes 327712 | tf_op jit(solution)/shard_map/while/body/eval_jaxpr/ppermute | solution.py:16
  51.9 0.3 fusion.48
  52.2 0.1 fusion.49
  52.4 0.5 convolution_add_fusion.3
  52.9 3.9 %collective-permute-start = (bf16[2,128,640]{1,2,0:T(8,128)(2,1)S(1)}, bf16[2,128,640]{1,2,0:T(8,128)(2,1)S(1)}, u32[]{:S(2)}, u32[]{:S(2)}) collective-permute-start(bf16[2,128,640]{1,2,0:T(8,128)(2,1)S(1)} %get-tuple-element.506), channel_id=1, source_target_pairs={{0,1},{1,2},{2,3},{3,4},{4,5},{5,6},{6,7},{7,8},{8,9},{9,10},{10,1... | collective-permute-start | bytes 983048 | tf_op jit(solution)/shard_map/while/body/eval_jaxpr/ppermute | solution.py:16
  56.8 2.9 %collective-permute-start.1 = (bf16[2,128,640]{1,2,0:T(8,128)(2,1)S(1)}, bf16[2,128,640]{1,2,0:T(8,128)(2,1)S(1)}, u32[]{:S(2)}, u32[]{:S(2)}) collective-permute-start(bf16[2,128,640]{1,2,0:T(8,128)(2,1)S(1)} %get-tuple-element.507), channel_id=1, source_target_pairs={{1,0},{2,1},{3,2},{4,3},{5,4},{6,5},{7,6},{8,7},{9,8},{10,9},{11,1... | collective-permute-start | bytes 983048 | tf_op jit(solution)/shard_map/while/body/eval_jaxpr/ppermute | solution.py:16
  59.8 1.3 gather_fusion
  61.2 0.1 and_reduce_fusion.3
  61.5 3.3 %collective-permute-done = bf16[2,128,640]{1,2,0:T(8,128)(2,1)S(1)} collective-permute-done((bf16[2,128,640]{1,2,0:T(8,128)(2,1)S(1)}, bf16[2,128,640]{1,2,0:T(8,128)(2,1)S(1)}, u32[]{:S(2)}, u32[]{:S(2)}) %collective-permute-start) | collective-permute-done | bytes 327712 | tf_op jit(solution)/shard_map/while/body/eval_jaxpr/ppermute | solution.py:16
  64.8 0.5 collective-permute-done.1
  65.4 0.3 fusion.48
  65.7 0.1 fusion.49
  65.9 0.5 convolution_add_fusion.3
  66.4 0.2 copy.61
  66.7 46.1 %all-gather.2.cloned.1.call-done = bf16[640,5120]{0,1:T(8,128)(2,1)} async-done(((bf16[640,80]{0,1:T(8,128)(2,1)}), bf16[640,5120]{0,1:T(8,128)(2,1)}) %all-gather.2.cloned.1.call-update) | async-done | bytes 6553616 | tf_op jit(solution)/shard_map/all_gather | solution.py:28
  112.7 5.1 %fusion.12 = bf16[5120,128]{0,1:T(8,128)(2,1)S(1)} fusion(bf16[128,640]{0,1:T(8,128)(2,1)S(1)} %bitcast.78, bf16[640,5120]{0,1:T(8,128)(2,1)} %all-gather.2.cloned.1.call-done), kind=kOutput, calls=%fused_computation.29 | convolution fusion | flops 839516160 | bytes 8028160 | tf_op jit(solution)/shard_map/dot_general | solution.py:93
  117.8 1.5 copy.70
  119.3 43.5 %reduce-scatter.4.cloned.1.call-done = bf16[640,128]{1,0:T(8,128)(2,1)} async-done(((bf16[5120,128]{1,0:T(8,128)(2,1)}), bf16[640,128]{1,0:T(8,128)(2,1)}) %reduce-scatter.4.cloned.1.call-update) | async-done | bytes 163856
  162.8 1.1 copy.71
  163.9 0.8 copy.62
  (55 shorter events, 1.9 us)
Async XLA Ops:
  6.5 4.1 %copy-start = (s32[64,4]{0,1:T(4,128)S(1)}, s32[64,4]{0,1:T(4,128)}, u32[]{:S(2)}) copy-start(s32[64,4]{0,1:T(4,128)} %param.16) | copy-start | bytes 3076
  6.5 106.2 %all-gather.2.cloned.1.call-start = ((), (), s32[]{:S(2)}) async-start(), calls=%async_computation.1 | async-start | bytes 6656000 | tf_op jit(solution)/shard_map/all_gather | solution.py:28
  7.3 155.5 %reduce-scatter.4.cloned.1.call-start = ((), (), s32[]{:S(2)}) async-start(), calls=%async_computation.2 | async-start | bytes 1474560
  17.5 10.2 %collective-permute-start = (bf16[2,128,640]{1,2,0:T(8,128)(2,1)S(1)}, bf16[2,128,640]{1,2,0:T(8,128)(2,1)S(1)}, u32[]{:S(2)}, u32[]{:S(2)}) collective-permute-start(bf16[2,128,640]{1,2,0:T(8,128)(2,1)S(1)} %get-tuple-element.506), channel_id=1, source_target_pairs={{0,1},{1,2},{2,3},{3,4},{4,5},{5,6},{6,7},{7,8},{8,9},{9,10},{10,1... | collective-permute-start | bytes 983048 | tf_op jit(solution)/shard_map/while/body/eval_jaxpr/ppermute | solution.py:16
  19.5 13.6 %collective-permute-start.1 = (bf16[2,128,640]{1,2,0:T(8,128)(2,1)S(1)}, bf16[2,128,640]{1,2,0:T(8,128)(2,1)S(1)}, u32[]{:S(2)}, u32[]{:S(2)}) collective-permute-start(bf16[2,128,640]{1,2,0:T(8,128)(2,1)S(1)} %get-tuple-element.507), channel_id=1, source_target_pairs={{1,0},{2,1},{3,2},{4,3},{5,4},{6,5},{7,6},{8,7},{9,8},{10,9},{11,1... | collective-permute-start | bytes 983048 | tf_op jit(solution)/shard_map/while/body/eval_jaxpr/ppermute | solution.py:16
  34.2 12.2 %collective-permute-start = (bf16[2,128,640]{1,2,0:T(8,128)(2,1)S(1)}, bf16[2,128,640]{1,2,0:T(8,128)(2,1)S(1)}, u32[]{:S(2)}, u32[]{:S(2)}) collective-permute-start(bf16[2,128,640]{1,2,0:T(8,128)(2,1)S(1)} %get-tuple-element.506), channel_id=1, source_target_pairs={{0,1},{1,2},{2,3},{3,4},{4,5},{5,6},{6,7},{7,8},{8,9},{9,10},{10,1... | collective-permute-start | bytes 983048 | tf_op jit(solution)/shard_map/while/body/eval_jaxpr/ppermute | solution.py:16
  40.7 11.0 %collective-permute-start.1 = (bf16[2,128,640]{1,2,0:T(8,128)(2,1)S(1)}, bf16[2,128,640]{1,2,0:T(8,128)(2,1)S(1)}, u32[]{:S(2)}, u32[]{:S(2)}) collective-permute-start(bf16[2,128,640]{1,2,0:T(8,128)(2,1)S(1)} %get-tuple-element.507), channel_id=1, source_target_pairs={{1,0},{2,1},{3,2},{4,3},{5,4},{6,5},{7,6},{8,7},{9,8},{10,9},{11,1... | collective-permute-start | bytes 983048 | tf_op jit(solution)/shard_map/while/body/eval_jaxpr/ppermute | solution.py:16
  52.9 11.8 %collective-permute-start = (bf16[2,128,640]{1,2,0:T(8,128)(2,1)S(1)}, bf16[2,128,640]{1,2,0:T(8,128)(2,1)S(1)}, u32[]{:S(2)}, u32[]{:S(2)}) collective-permute-start(bf16[2,128,640]{1,2,0:T(8,128)(2,1)S(1)} %get-tuple-element.506), channel_id=1, source_target_pairs={{0,1},{1,2},{2,3},{3,4},{4,5},{5,6},{6,7},{7,8},{8,9},{9,10},{10,1... | collective-permute-start | bytes 983048 | tf_op jit(solution)/shard_map/while/body/eval_jaxpr/ppermute | solution.py:16
  56.8 8.5 %collective-permute-start.1 = (bf16[2,128,640]{1,2,0:T(8,128)(2,1)S(1)}, bf16[2,128,640]{1,2,0:T(8,128)(2,1)S(1)}, u32[]{:S(2)}, u32[]{:S(2)}) collective-permute-start(bf16[2,128,640]{1,2,0:T(8,128)(2,1)S(1)} %get-tuple-element.507), channel_id=1, source_target_pairs={{1,0},{2,1},{3,2},{4,3},{5,4},{6,5},{7,6},{8,7},{9,8},{10,9},{11,1... | collective-permute-start | bytes 983048 | tf_op jit(solution)/shard_map/while/body/eval_jaxpr/ppermute | solution.py:16
  66.6 97.3 %copy-start.1 = (f32[640]{0:T(1024)S(1)}, f32[640]{0:T(1024)}, u32[]{:S(2)}) copy-start(f32[640]{0:T(1024)} %param.14) | copy-start | bytes 7684
Sparse Core Ops, SparseCore 0:
  10.6 102.0 all-gather.1
  119.4 43.3 reduce-scatter.3
where the time goes:
time: 172 us
  waiting for transfers between devices  109 us (63%)
  starting transfers between devices  21.7 us (13%)
  between operations  16 us (9%)
  local copies, waits for them, and re-layouts  14.6 us (8%)
  matrix products  7.99 us (5%)
  other arithmetic  2.42 us (1%)
    all_gather x1, waiting for transfers between devices, on_device(): weight_full = lax.all_gather(out_weight, 'seq', axis=1, tiled=True)  46.1 us
    unnamed x3, waiting for transfers between devices  44.2 us
    ppermute x6, starting transfers between devices, shifted(): return lax.ppermute(block, axis, route)  21.7 us
    ppermute x6, waiting for transfers between devices, shifted(): return lax.ppermute(block, axis, route)  18.3 us
    unnamed x12, local copies, waits for them, and re-layouts  6.06 us
    gather x4, local copies, waits for them, and re-layouts, absorb(): key_ids = jnp.take(tile_map, safe_slots)  5.27 us
    dot_general x1, matrix products, on_device(): lax.dot_general(weight_full, attention, (((0,), (1,)), ((), ())), preferr...  5.12 us
  transfers between devices with their start and end apart: 8, of which 8 were waited for; matrix products, arithmetic and copies ran while one was open for 10% of the time, Pallas kernels for 0%

commit v1 on v0

v1 whole, which is shorter than its diff:
```python
import functools
import jax
import jax.numpy as jnp
from jax import lax
from jax.experimental import pallas as pl
from jax.experimental.pallas import tpu as pltpu
from jax.sharding import PartitionSpec as P

HD = 128
TILE = 128
KMAX = 4
NX, NYL, NZ, NYH = 4, 2, 8, 4
PLANES = NZ * NYH
NEG = -1e30
HALVES = ((0, 48), (48, 32))
MESH = pl.DeviceIdType.MESH


def plus_hops(piece, half):
    return 4 if (piece + half) % 2 == 0 else 3


def kernel(
    q_ref, k_ref, v_ref, w_ref, gate_ref, map_ref, list_ref, count_ref, out_ref,
    kbuf, vbuf, wall, attn, obuf, xbuf, sbuf, fbuf, gcol, send_sems, recv_sems,
):
    heads = q_ref.shape[1] // HD
    wcols = w_ref.shape[0]
    f = lax.axis_index("fsdp")
    s = lax.axis_index("seq")
    yl, x = f // NX, f % NX
    core, yh, z = s % 2, (s // 2) % NYH, s // 8
    plane = s // 2

    def seq_id(zz, yy, cc):
        return zz * 8 + yy * 2 + cc

    def wrap(a, n):
        return (a + n) % n

    sibling = (f, seq_id(z, yh, 1 - core))
    z_next = (f, seq_id(wrap(z + 1, NZ), yh, core))
    z_prev = (f, seq_id(wrap(z - 1, NZ), yh, core))
    y_next = (f, seq_id(z, wrap(yh + 1, NYH), core))
    y_prev = (f, seq_id(z, wrap(yh - 1, NYH), core))
    p_next = (f, wrap(plane + 1, PLANES) * 2 + core)
    p_prev = (f, wrap(plane - 1, PLANES) * 2 + core)
    x_peer = [(yl * NX + wrap(x + r, NX), s) for r in range(NX)]
    y_same = ((1 - yl) * NX + x, s)
    y_cross = ((1 - yl) * NX + x, seq_id(z, yh, 1 - core))

    peers = [sibling, z_next, z_prev, y_next, y_prev, p_next, p_prev,
             x_peer[1], x_peer[2], x_peer[3], y_same, y_cross]
    barrier = pltpu.get_barrier_semaphore()
    for peer in peers:
        pl.semaphore_signal(barrier, inc=1, device_id=peer, device_id_type=MESH)

    kbuf[0] = k_ref[...]
    vbuf[0] = v_ref[...]
    wall[0, z] = w_ref[...]
    rows = lax.broadcasted_iota(jnp.int32, (HD, HD), 0)
    cols = lax.broadcasted_iota(jnp.int32, (HD, HD), 1)
    for i in range(gate_ref.shape[1] // HD):
        line = jnp.broadcast_to(gate_ref[:, i * HD:(i + 1) * HD], (HD, HD))
        column = jnp.sum(jnp.where(rows == cols, line, 0.0), axis=1, keepdims=True)
        gcol[i * HD:(i + 1) * HD, :] = jnp.broadcast_to(column, (HD, HD))

    pl.semaphore_wait(barrier, len(peers))

    started = []
    table = {}

    def number(key):
        return table.setdefault(key, len(table))

    def send(key, src, dst, peer):
        n = number(key)
        copy = pltpu.make_async_remote_copy(
            src_ref=src, dst_ref=dst, send_sem=send_sems.at[n], recv_sem=recv_sems.at[n],
            device_id=peer, device_id_type=MESH,
        )
        copy.start()
        started.append(copy)

    def receive(key, dst):
        n = number(key)
        pltpu.make_async_remote_copy(
            src_ref=dst, dst_ref=dst, send_sem=send_sems.at[n], recv_sem=recv_sems.at[n],
            device_id=sibling, device_id_type=MESH,
        ).wait_recv()

    def part(piece, zz, half):
        start, size = HALVES[half]
        return wall.at[piece, zz, pl.ds(start, size)]

    def ring_pieces(hop):
        return ((0, wrap(z - hop, NZ)), (1, wrap(z + hop, NZ)))

    def hops(piece, half, way):
        n = plus_hops(piece, half)
        return n if way == 0 else NZ - 1 - n

    def ring_receive(piece, hop):
        for half in range(2):
            for way, zz in ring_pieces(hop):
                if hop <= hops(piece, half, way):
                    receive(("z", piece, half, way, hop), part(piece, zz, half))

    def ring_step(piece, hop):
        for half in range(2):
            for way, zz in ring_pieces(hop - 1):
                last = hops(piece, half, way)
                if hop > 1 and hop - 1 <= last:
                    receive(("z", piece, half, way, hop - 1), part(piece, zz, half))
                if hop <= last:
                    ref = part(piece, zz, half)
                    send(("z", piece, half, way, hop), ref, ref, (z_next, z_prev)[way])

    def ring_last(piece):
        for half in range(2):
            for way in range(2):
                if hops(piece, half, way) == 4:
                    zz = ring_pieces(4)[way][1]
                    receive(("z", piece, half, way, 4), part(piece, zz, half))

    send(("y", 1), w_ref, wall.at[1, z], y_next)
    send(("y", 2), w_ref, wall.at[2, z], y_prev)
    ring_step(0, 1)
    send("ksib", k_ref, kbuf.at[1], sibling)
    send("vsib", v_ref, vbuf.at[1], sibling)
    send("kup", k_ref, kbuf.at[2], p_next)
    send("kdown", k_ref, kbuf.at[4], p_prev)
    send("vup", v_ref, vbuf.at[2], p_next)
    send("vdown", v_ref, vbuf.at[4], p_prev)

    def forward(name, buf):
        receive(name + "up", buf.at[2])
        send(name + "upfwd", buf.at[2], buf.at[3], sibling)
        receive(name + "down", buf.at[4])
        send(name + "downfwd", buf.at[4], buf.at[5], sibling)

    def attention_wait():
        for name, buf in (("k", kbuf), ("v", vbuf)):
            receive(name + "sib", buf.at[1])
            receive(name + "upfwd", buf.at[3])
            receive(name + "downfwd", buf.at[5])

    def key_bias():
        tile = map_ref[s]
        used = count_ref[tile]
        listed = [list_ref[tile, i] for i in range(KMAX)]
        below, above = wrap(plane - 1, PLANES), wrap(plane + 1, PLANES)
        slots = (
            (s, None), (plane * 2 + 1 - core, None),
            (below * 2 + core, plane > 0), (below * 2 + 1 - core, plane > 0),
            (above * 2 + core, plane < PLANES - 1), (above * 2 + 1 - core, plane < PLANES - 1),
        )
        lane_tile = lax.broadcasted_iota(jnp.int32, (1, 6 * TILE), 1) // TILE
        bias = jnp.zeros((1, 6 * TILE), jnp.float32)
        for n, (slot, inside) in enumerate(slots):
            other = map_ref[slot]
            hit = jnp.int32(0)
            for i in range(KMAX):
                same = jnp.where(listed[i] == other, 1, 0) * jnp.where(used > i, 1, 0)
                hit = jnp.maximum(hit, same)
            if inside is not None:
                hit = hit * jnp.where(inside, 1, 0)
            value = jnp.where(hit == 1, 0.0, NEG).astype(jnp.float32)
            bias = jnp.where(lane_tile == n, value, bias)
        return bias

    def attention_head(h, bias):
        span = slice(h * HD, (h + 1) * HD)
        keys = kbuf[:, :, span].reshape(6 * TILE, HD)
        values = vbuf[:, :, span].reshape(6 * TILE, HD)
        scores = lax.dot_general(
            q_ref[:, span], keys, (((1,), (1,)), ((), ())), preferred_element_type=jnp.float32
        )
        scores = scores * (1.0 / float(HD) ** 0.5) + bias
        top = jnp.max(scores, axis=1, keepdims=True)
        expo = jnp.exp(scores - top)
        total = jnp.sum(expo, axis=1, keepdims=True)
        mixed = jnp.dot(expo.astype(jnp.bfloat16), values, preferred_element_type=jnp.float32)
        attn[core, :, span] = (mixed / total).astype(jnp.bfloat16)

    def project(piece):
        weights = wall[piece].reshape(NZ * wcols, heads * HD)
        tokens = attn[...].reshape(2 * TILE, heads * HD)
        partial = lax.dot_general(
            weights, tokens, (((1,), (1,)), ((), ())), preferred_element_type=jnp.float32
        ).astype(jnp.bfloat16)
        for b in range(NZ):
            obuf[piece, b % NX, b // NX] = partial[b * wcols:(b + 1) * wcols]
        for r in (2, 1, 3):
            send(("x", piece, r), obuf.at[piece, wrap(x + r, NX)], xbuf.at[piece, r - 1], x_peer[r])

    def reduce_x(piece):
        total = obuf[piece, x].astype(jnp.float32)
        for r in (1, 3, 2):
            receive(("x", piece, r), xbuf.at[piece, r - 1])
            total = total + xbuf[piece, r - 1].astype(jnp.float32)
        total = total.astype(jnp.bfloat16)
        for t in range(2):
            sbuf[piece, :, t] = total[:, :, t * TILE:(t + 1) * TILE]
        send(("f", piece, 1), sbuf.at[piece, 1 - yl, core], fbuf.at[piece, 1], y_same)
        send(("f", piece, 2), sbuf.at[piece, 1 - yl, 1 - core], fbuf.at[piece, 2], y_cross)
        send(("f", piece, 3), sbuf.at[piece, yl, 1 - core], fbuf.at[piece, 0], sibling)

    def finish(piece):
        receive(("f", piece, 1), fbuf.at[piece, 1])
        receive(("f", piece, 2), fbuf.at[piece, 2])
        receive(("f", piece, 3), fbuf.at[piece, 0])
        from_yh = wrap(yh + (0, -1, 1, 2)[piece], NYH)
        for other in range(2):
            c = core if other == 0 else 1 - core
            start = pl.multiple_of(from_yh * (2 * wcols) + c * wcols, 16)
            near = sbuf[piece, yl, core] if other == 0 else fbuf[piece, 0]
            far = fbuf[piece, 1] if other == 0 else fbuf[piece, 2]
            summed = near.astype(jnp.float32) + far.astype(jnp.float32)
            gate = gcol[pl.ds(start, wcols), :]
            out_ref[pl.ds(start, wcols), :] = (gate * summed).astype(out_ref.dtype)

    ring_step(0, 2)
    ring_step(0, 3)
    receive(("y", 1), wall.at[1, z])
    ring_step(1, 1)
    start, size = HALVES[0]
    send(("y", 3), wall.at[1, z, pl.ds(start, size)], wall.at[3, z, pl.ds(start, size)], y_next)
    ring_step(0, 4)
    receive(("y", 2), wall.at[2, z])
    start, size = HALVES[1]
    send(("y", 4), wall.at[2, z, pl.ds(start, size)], wall.at[3, z, pl.ds(start, size)], y_prev)
    ring_step(1, 2)
    forward("k", kbuf)
    ring_step(1, 3)
    ring_step(2, 1)
    ring_step(1, 4)
    forward("v", vbuf)
    ring_step(2, 2)
    bias = key_bias()
    attention_wait()
    for h in range(heads):
        attention_head(h, bias)
        if h == 2:
            ring_step(2, 3)
    send("attn", attn.at[core], attn.at[core], sibling)
    for half in range(2):
        start, size = HALVES[half]
        receive(("y", 3 + half), wall.at[3, z, pl.ds(start, size)])
    ring_step(3, 1)
    ring_step(2, 4)
    ring_last(0)
    receive("attn", attn.at[1 - core])
    project(0)
    ring_step(3, 2)
    ring_last(1)
    project(1)
    reduce_x(0)
    ring_step(3, 3)
    ring_last(2)
    project(2)
    reduce_x(1)
    finish(0)
    ring_step(3, 4)
    reduce_x(2)
    finish(1)
    ring_last(3)
    project(3)
    finish(2)
    reduce_x(3)
    finish(3)
    for copy in started:
        copy.wait_send()


def on_device(q_heads, k_heads, v_heads, out_weight, out_gate, tile_map, key_tiles, key_count):
    tokens, width = q_heads.shape
    wcols = out_weight.shape[1]
    features = out_gate.shape[0]
    vmem = pl.BlockSpec(memory_space=pltpu.VMEM)
    smem = pl.BlockSpec(memory_space=pltpu.SMEM)
    bf16 = jnp.bfloat16
    return pl.pallas_call(
        kernel,
        out_shape=jax.ShapeDtypeStruct((features, tokens), bf16),
        in_specs=[vmem] * 5 + [smem] * 3,
        out_specs=vmem,
        scratch_shapes=[
            pltpu.VMEM((6, TILE, width), bf16),
            pltpu.VMEM((6, TILE, width), bf16),
            pltpu.VMEM((4, NZ, wcols, width), bf16),
            pltpu.VMEM((2, TILE, width), bf16),
            pltpu.VMEM((4, NX, NYL, wcols, 2 * TILE), bf16),
            pltpu.VMEM((4, NX - 1, NYL, wcols, 2 * TILE), bf16),
            pltpu.VMEM((4, NYL, 2, wcols, TILE), bf16),
            pltpu.VMEM((4, 3, wcols, TILE), bf16),
            pltpu.VMEM((features, HD), jnp.float32),
            pltpu.SemaphoreType.DMA((104,)),
            pltpu.SemaphoreType.DMA((104,)),
        ],
        compiler_params=pltpu.CompilerParams(
            collective_id=0, has_side_effects=True, vmem_limit_bytes=32 * 2**20
        ),
        cost_estimate=pl.CostEstimate(
            flops=1_100_000_000, bytes_accessed=2_000_000, transcendentals=500_000
        ),
        name="attend_project",
    )(q_heads, k_heads, v_heads, out_weight.T, out_gate.reshape(1, features),
      tile_map, key_tiles, key_count)


def solution(mesh):
    return jax.shard_map(
        on_device,
        mesh=mesh,
        in_specs=(
            P("seq", "fsdp"),
            P("seq", "fsdp"),
            P("seq", "fsdp"),
            P("fsdp", "seq"),
            P("fsdp"),
            P(),
            P(),
            P(),
        ),
        out_specs=P("fsdp", "seq"),
        check_vma=False,
    )
```

time: 172 us -> 83 us (0.48)
  the two profiles are of different devices: /device:TPU:16 before, /device:TPU:1 now
where the time goes in v1:
time: 83 us; the launch traced here: 81.9 us
  Pallas kernels  76.2 us (92%)
  local copies, waits for them, and re-layouts  5.68 us (7%)
    pallas_call x1, Pallas kernels, on_device(): pl.pallas_call(kernel, out_shape=jax.ShapeDtypeStruct((features, tokens),...  76.2 us
    unnamed x16, local copies, waits for them, and re-layouts  4.98 us

profile of v1, /device:TPU:1, one launch (start us, length us, event | category | flops | bytes accessed | tf_op | source)
XLA Modules:
  0.0 81.9 jit_solution(8574604634413478450)
XLA Ops:
  0.0 0.0 copy-start.6
  0.0 0.7 reshape.3.gate_ref
  0.7 0.0 copy-done.6
  0.7 0.0 copy-start.4
  0.7 0.0 copy-start.5
  0.7 0.1 copy.9.list_ref
  0.8 0.6 copy-done.4
  1.4 0.0 copy-done.5
  1.4 0.0 copy-start
  1.4 0.9 %copy-done = bf16[128,640]{1,0:T(8,128)(2,1)S(1)} copy-done((bf16[128,640]{1,0:T(8,128)(2,1)S(1)}, bf16[128,640]{1,0:T(8,128)(2,1)}, u32[]{:S(2)}) %copy-start) | copy-done | bytes 163864
  2.3 0.0 copy-start.1
  2.3 0.9 %copy-done.1 = bf16[128,640]{1,0:T(8,128)(2,1)S(1)} copy-done((bf16[128,640]{1,0:T(8,128)(2,1)S(1)}, bf16[128,640]{1,0:T(8,128)(2,1)}, u32[]{:S(2)}) %copy-start.1) | copy-done | bytes 163864
  3.2 0.0 copy-start.2
  3.2 0.9 %copy-done.2 = bf16[128,640]{1,0:T(8,128)(2,1)S(1)} copy-done((bf16[128,640]{1,0:T(8,128)(2,1)S(1)}, bf16[128,640]{1,0:T(8,128)(2,1)}, u32[]{:S(2)}) %copy-start.2) | copy-done | bytes 163864
  4.1 0.0 copy-start.3
  4.1 0.9 %copy-done.3 = bf16[640,80]{0,1:T(8,128)(2,1)S(1)} copy-done((bf16[640,80]{0,1:T(8,128)(2,1)S(1)}, bf16[640,80]{0,1:T(8,128)(2,1)}, u32[]{:S(2)}) %copy-start.3) | copy-done | bytes 102424
  5.0 76.2 %attend_project.1 = bf16[640,128]{1,0:T(8,128)(2,1)S(1)} custom-call(bf16[128,640]{1,0:T(8,128)(2,1)S(1)} %copy-done, bf16[128,640]{1,0:T(8,128)(2,1)S(1)} %copy-done.1, bf16[128,640]{1,0:T(8,128)(2,1)S(1)} %copy-done.2, bf16[80,640]{1,0:T(8,128)(2,1)S(1)} %bitcast.1, f32[1,640]{1,0:T(1,128)S(1)} %reshape.3.gate_ref, s32[64]{0:T(128)S(1)} %copy-done.4, ...), custom_call_target="tpu_custom_call" | custom-call | flops 1100000000 | bytes 2000000 | tf_op jit(solution)/shard_map/attend_project/pallas_call | solution.py:283
  81.2 0.7 copy.11
Async XLA Ops:
  0.0 0.7 copy-start.6
  0.7 0.7 copy-start.4
  0.7 0.7 copy-start.5
  1.4 0.9 %copy-start = (bf16[128,640]{1,0:T(8,128)(2,1)S(1)}, bf16[128,640]{1,0:T(8,128)(2,1)}, u32[]{:S(2)}) copy-start(bf16[128,640]{1,0:T(8,128)(2,1)} %q_ref.1) | copy-start | bytes 491524
  2.3 0.9 %copy-start.1 = (bf16[128,640]{1,0:T(8,128)(2,1)S(1)}, bf16[128,640]{1,0:T(8,128)(2,1)}, u32[]{:S(2)}) copy-start(bf16[128,640]{1,0:T(8,128)(2,1)} %k_ref.1) | copy-start | bytes 491524
  3.2 0.9 %copy-start.2 = (bf16[128,640]{1,0:T(8,128)(2,1)S(1)}, bf16[128,640]{1,0:T(8,128)(2,1)}, u32[]{:S(2)}) copy-start(bf16[128,640]{1,0:T(8,128)(2,1)} %v_ref.1) | copy-start | bytes 491524
  4.1 0.9 %copy-start.3 = (bf16[640,80]{0,1:T(8,128)(2,1)S(1)}, bf16[640,80]{0,1:T(8,128)(2,1)}, u32[]{:S(2)}) copy-start(bf16[640,80]{0,1:T(8,128)(2,1)} %param.11) | copy-start | bytes 307204

commit v2 on v1

v2 whole, which is shorter than its diff:
```python
import functools
import jax
import jax.numpy as jnp
from jax import lax
from jax.experimental import pallas as pl
from jax.experimental.pallas import tpu as pltpu
from jax.sharding import PartitionSpec as P

HD = 128
TILE = 128
KMAX = 4
NX, NYL, NZ, NYH = 4, 2, 8, 4
PLANES = NZ * NYH
NEG = -1e30
HALVES = ((0, 48), (48, 32))
MESH = pl.DeviceIdType.MESH


FEW = (1, 1)
ORDER = (2, 6, 1, 7, 3, 5, 4)
CHUNKS = ((0, 3), (3, 2))
OFFSETS = ((0, 0), (-1, 1), (1, -1), (2, 2))


def kernel(
    q_ref, k_ref, v_ref, w_ref, gate_ref, map_ref, list_ref, count_ref, out_ref,
    qbuf, kv, wtmp, wall, attn, toks, keep, give, take, sbuf, rbuf, gline, gcol,
    tile_map, key_list, key_count, local_sems, send_sems, recv_sems,
):
    heads = q_ref.shape[1] // HD
    wcols = w_ref.shape[0]
    f = lax.axis_index("fsdp")
    s = lax.axis_index("seq")
    yl, x = f // NX, f % NX
    core, yh, z = s % 2, (s // 2) % NYH, s // 8
    plane = s // 2

    def seq_id(zz, yy, cc):
        return zz * 8 + yy * 2 + cc

    def wrap(a, n):
        return (a + n) % n

    sibling = (f, seq_id(z, yh, 1 - core))
    z_next = (f, seq_id(wrap(z + 1, NZ), yh, core))
    z_prev = (f, seq_id(wrap(z - 1, NZ), yh, core))
    y_next = (f, seq_id(z, wrap(yh + 1, NYH), core))
    y_prev = (f, seq_id(z, wrap(yh - 1, NYH), core))
    p_next = (f, wrap(plane + 1, PLANES) * 2 + core)
    p_prev = (f, wrap(plane - 1, PLANES) * 2 + core)
    kind = ((x + 1) // 2) % 2
    own = core == kind
    mate = yl * NX + x + 1 - 2 * (x % 2)
    swap_peer = (mate, seq_id(z, yh, 1 - core))
    mate_core = (mate, seq_id(z, yh, kind))
    groups = NX * NYL
    fsdp_peer = [(wrap(f + r, groups), s) for r in range(groups)]

    peers = [sibling, z_next, z_prev, y_next, y_prev, p_next, p_prev, swap_peer] + fsdp_peer[1:]
    local = [
        pltpu.make_async_copy(src, dst, local_sems.at[n])
        for n, (src, dst) in enumerate((
            (w_ref, wtmp), (k_ref, kv.at[0, 0]), (v_ref, kv.at[0, 1]), (q_ref, qbuf),
            (gate_ref, gline), (map_ref, tile_map), (list_ref, key_list), (count_ref, key_count),
        ))
    ]
    for copy in local:
        copy.start()
    barrier = pltpu.get_barrier_semaphore()
    for peer in peers:
        pl.semaphore_signal(barrier, inc=1, device_id=peer, device_id_type=MESH)

    def gate_column():
        local[4].wait()
        rows = lax.broadcasted_iota(jnp.int32, (HD, HD), 0)
        cols = lax.broadcasted_iota(jnp.int32, (HD, HD), 1)
        for i in range(gline.shape[0] // HD):
            line = jnp.broadcast_to(gline[i * HD:(i + 1) * HD].reshape(1, HD), (HD, HD))
            column = jnp.sum(jnp.where(rows == cols, line, 0.0), axis=1, keepdims=True)
            gcol[i * HD:(i + 1) * HD, :] = jnp.broadcast_to(column, (HD, HD))

    for copy in local[:4]:
        copy.wait()
    pl.semaphore_wait(barrier, len(peers))

    started = []
    table = {}

    def number(key):
        return table.setdefault(key, len(table))

    def send(key, src, dst, peer):
        n = number(key)
        copy = pltpu.make_async_remote_copy(
            src_ref=src, dst_ref=dst, send_sem=send_sems.at[n], recv_sem=recv_sems.at[n],
            device_id=peer, device_id_type=MESH,
        )
        copy.start()
        started.append(copy)

    def receive(key, dst):
        n = number(key)
        pltpu.make_async_remote_copy(
            src_ref=dst, dst_ref=dst, send_sem=send_sems.at[n], recv_sem=recv_sems.at[n],
            device_id=sibling, device_id_type=MESH,
        ).wait_recv()

    def swap():
        n = number("swap")
        copy = pltpu.make_async_remote_copy(
            src_ref=wtmp, dst_ref=wall.at[0, z], send_sem=send_sems.at[n],
            recv_sem=recv_sems.at[n], device_id=swap_peer, device_id_type=MESH,
        )

        @pl.when(own)
        def _():
            wall[0, z] = wtmp[...]

        @pl.when(jnp.logical_not(own))
        def _():
            copy.start()
            copy.wait()

    def part(piece, zz, half):
        start, size = HALVES[half]
        return wall.at[piece, zz, pl.ds(start, size)]

    def ring_pieces(hop):
        return (wrap(z - hop, NZ), wrap(z + hop, NZ))

    def last_way(piece, half):
        inner = (piece + half) % 2
        low, high = (0, 1) if (piece, half) == FEW else (1, 0)
        return jnp.where(yh == 0, low, jnp.where(yh == NYH - 1, high, inner))

    def ring_step(piece, hop):
        for half in range(2):
            if hop > 1:
                for way, zz in enumerate(ring_pieces(hop - 1)):
                    receive(("z", piece, half, way, hop - 1), part(piece, zz, half))
                    if hop < 4:
                        ref = part(piece, zz, half)
                        send(("z", piece, half, way, hop), ref, ref, (z_next, z_prev)[way])
            else:
                for way in range(2):
                    ref = part(piece, z, half)
                    send(("z", piece, half, way, 1), ref, ref, (z_next, z_prev)[way])
            if hop == 4:
                turn = 2 * last_way(piece, half) - 1
                ref = part(piece, wrap(z + 3 * turn, NZ), half)
                peer = (f, seq_id(wrap(z - turn, NZ), yh, core))
                send(("z", piece, half, 4), ref, ref, peer)

    def ring_last(piece, halves=(0, 1)):
        for half in halves:
            receive(("z", piece, half, 4), part(piece, wrap(z + 4, NZ), half))

    def rows(piece, half):
        return part(piece, z, half)

    def weights_out(piece):
        for half in range(2):
            peer = y_next if (half == 0) == (piece == 1) else y_prev
            send(("y", piece, half), rows(0, half), rows(piece, half), peer)

    def weights_in(piece):
        for half in range(2):
            receive(("y", piece, half), rows(piece, half))

    def weights_on():
        for half, peer in ((0, y_next), (1, y_prev)):
            send(("y", 3, half), rows(1, half), rows(3, half), peer)

    def sibling_out():
        send(("s",), kv.at[0], kv.at[1], sibling)

    def heads_of(slot, chunk):
        start, size = CHUNKS[chunk]
        return kv.at[slot, :, :, pl.ds(start * HD, size * HD)]

    def halo(chunk):
        send(("h", chunk, 0), heads_of(0, chunk), heads_of(2, chunk), p_next)
        send(("h", chunk, 1), heads_of(0, chunk), heads_of(4, chunk), p_prev)

    def forward(chunk):
        for way, slot in ((0, 2), (1, 4)):
            receive(("h", chunk, way), heads_of(slot, chunk))
            send(("g", chunk, way), heads_of(slot, chunk), heads_of(slot + 1, chunk), sibling)

    def key_bias():
        for copy in local[5:]:
            copy.wait()
        tile = tile_map[s]
        used = key_count[tile]
        listed = [key_list[i, tile] for i in range(KMAX)]
        below, above = wrap(plane - 1, PLANES), wrap(plane + 1, PLANES)
        slots = (
            (s, None), (plane * 2 + 1 - core, None),
            (below * 2 + core, plane > 0), (below * 2 + 1 - core, plane > 0),
            (above * 2 + core, plane < PLANES - 1), (above * 2 + 1 - core, plane < PLANES - 1),
        )
        lane_tile = lax.broadcasted_iota(jnp.int32, (1, 6 * TILE), 1) // TILE
        bias = jnp.zeros((1, 6 * TILE), jnp.float32)
        for n, (slot, inside) in enumerate(slots):
            other = tile_map[slot]
            hit = jnp.int32(0)
            for i in range(KMAX):
                same = jnp.where(listed[i] == other, 1, 0) * jnp.where(used > i, 1, 0)
                hit = jnp.maximum(hit, same)
            if inside is not None:
                hit = hit * jnp.where(inside, 1, 0)
            value = jnp.where(hit == 1, 0.0, NEG).astype(jnp.float32)
            bias = jnp.where(lane_tile == n, value, bias)
        return bias

    def attention_head(h, bias):
        span = slice(h * HD, (h + 1) * HD)
        keys = kv[:, 0, :, span].reshape(6 * TILE, HD)
        values = kv[:, 1, :, span].reshape(6 * TILE, HD)
        scores = lax.dot_general(
            qbuf[:, span], keys, (((1,), (1,)), ((), ())), preferred_element_type=jnp.float32
        )
        scores = scores * (1.0 / float(HD) ** 0.5) + bias
        top = jnp.max(scores, axis=1, keepdims=True)
        expo = jnp.exp(scores - top)
        total = jnp.sum(expo, axis=1, keepdims=True)
        mixed = jnp.dot(expo.astype(jnp.bfloat16), values, preferred_element_type=jnp.float32)
        attn[:, span] = (mixed / total).astype(jnp.bfloat16)

    def token_copy(name, chunk, slot, peer):
        n, m = number(("a", name, chunk)), number(("a", slot, chunk))
        start, size = CHUNKS[chunk]
        span = pl.ds(start * HD, size * HD)
        return pltpu.make_async_remote_copy(
            src_ref=attn.at[:, span], dst_ref=toks.at[slot, :, span], send_sem=send_sems.at[n],
            recv_sem=recv_sems.at[m], device_id=peer, device_id_type=MESH,
        )

    def attention(chunk, bias):
        for way, slot in ((0, 3), (1, 5)):
            receive(("g", chunk, way), heads_of(slot, chunk))
        start, size = CHUNKS[chunk]
        for h in range(start, start + size):
            attention_head(h, bias)

        @pl.when(own)
        def _():
            token_copy("mate", chunk, 0, mate_core).start()
            span = slice(start * HD, (start + size) * HD)
            toks[0, :, span] = attn[:, span]

        @pl.when(jnp.logical_not(own))
        def _():
            token_copy("mate", chunk, 1, mate_core).start()
            token_copy("sib", chunk, 1, sibling).start()

    def tokens_in(chunk):
        @pl.when(jnp.logical_not(own))
        def _():
            token_copy(0, chunk, 0, sibling).wait_recv()

        token_copy(1, chunk, 1, sibling).wait_recv()

    def tokens_end(chunk):
        token_copy("mate", chunk, 1, mate_core).wait_send()

        @pl.when(jnp.logical_not(own))
        def _():
            token_copy("sib", chunk, 1, sibling).wait_send()

    def span_of(half):
        return (0, wcols) if half is None else HALVES[half]

    def project(piece, half=None):
        start, size = span_of(half)
        span = pl.ds(start, size)
        weights = wall[piece, :, span].reshape(NZ * size, heads * HD)
        tokens = toks[...].reshape(2 * TILE, heads * HD)
        partial = lax.dot_general(
            weights, tokens, (((1,), (1,)), ((), ())), preferred_element_type=jnp.float32
        )
        give[piece, :, span] = partial[:, TILE:].astype(jnp.bfloat16).reshape(NZ, size, TILE)
        send(("c", piece, half), give.at[piece, :, span], take.at[piece, :, span], sibling)
        keep[piece, :, span] = partial[:, :TILE].reshape(NZ, size, TILE)

    def scatter(piece, half=None):
        start, size = span_of(half)
        span = pl.ds(start, size)
        receive(("c", piece, half), take.at[piece, :, span])
        total = keep[piece, :, span] + take[piece, :, span].astype(jnp.float32)
        sbuf[piece, :, span] = total.astype(jnp.bfloat16)
        for r in ORDER:
            dst = rbuf.at[piece, f, span]
            to = fsdp_peer[r]
            send(("f", piece, half, r), sbuf.at[piece, to[0], span], dst, to)
        rbuf[piece, f, span] = sbuf[piece, f, span]

    def finish(piece, half=None):
        start, size = span_of(half)
        span = pl.ds(start, size)
        for r in ORDER:
            receive(("f", piece, half, r), rbuf.at[piece, wrap(f - r, groups), span])
        for part_half in range(2) if half is None else (half,):
            start, size = HALVES[part_half]
            span = pl.ds(start, size)
            from_yh = wrap(yh + OFFSETS[piece][part_half], NYH)
            for column_core, sources in ((0, (0, 3, 4, 7)), (1, (1, 2, 5, 6))):
                first = pl.multiple_of(from_yh * (2 * wcols) + column_core * wcols + start, 16)
                summed = jnp.zeros((size, TILE), jnp.float32)
                for source in sources:
                    summed = summed + rbuf[piece, source, span].astype(jnp.float32)
                gate = gcol[pl.ds(first, size), :]
                out_ref[pl.ds(first, size), :] = (gate * summed).astype(out_ref.dtype)

    swap()
    weights_out(1)
    ring_step(0, 1)
    weights_out(2)
    sibling_out()
    gate_column()
    bias = key_bias()
    ring_step(0, 2)
    halo(0)
    weights_in(1)
    weights_on()
    ring_step(1, 1)
    ring_step(0, 3)
    halo(1)
    ring_step(1, 2)
    ring_step(0, 4)
    weights_in(2)
    ring_step(2, 1)
    ring_step(1, 3)
    ring_step(2, 2)
    ring_step(1, 4)
    weights_in(3)
    ring_step(3, 1)
    forward(0)
    ring_step(2, 3)
    receive(("s",), kv.at[1])
    attention(0, bias)
    ring_step(3, 2)
    forward(1)
    ring_step(2, 4)
    attention(1, bias)
    ring_step(3, 3)
    ring_last(0)
    tokens_in(0)
    tokens_in(1)
    project(0)
    ring_last(1)
    project(1)
    scatter(0)
    ring_step(3, 4)
    scatter(1)
    ring_last(2)
    project(2)
    finish(0)
    scatter(2)
    ring_last(3, (0,))
    project(3, 0)
    ring_last(3, (1,))
    project(3, 1)
    finish(1)
    scatter(3, 0)
    scatter(3, 1)
    finish(2)
    finish(3, 0)
    finish(3, 1)
    tokens_end(0)
    tokens_end(1)
    for copy in started:
        copy.wait_send()


def on_device(q_heads, k_heads, v_heads, out_weight, out_gate, tile_map, key_tiles, key_count):
    tokens, width = q_heads.shape
    wcols = out_weight.shape[1]
    features = out_gate.shape[0]
    vmem = pl.BlockSpec(memory_space=pltpu.VMEM)
    bf16 = jnp.bfloat16
    return pl.pallas_call(
        kernel,
        out_shape=jax.ShapeDtypeStruct((features, tokens), bf16),
        in_specs=[pl.BlockSpec(memory_space=pl.ANY)] * 8,
        out_specs=vmem,
        scratch_shapes=[
            pltpu.VMEM((TILE, width), bf16),
            pltpu.VMEM((6, 2, TILE, width), bf16),
            pltpu.VMEM((wcols, width), bf16),
            pltpu.VMEM((4, NZ, wcols, width), bf16),
            pltpu.VMEM((TILE, width), bf16),
            pltpu.VMEM((2, TILE, width), bf16),
            pltpu.VMEM((4, NZ, wcols, TILE), jnp.float32),
            pltpu.VMEM((4, NZ, wcols, TILE), bf16),
            pltpu.VMEM((4, NZ, wcols, TILE), bf16),
            pltpu.VMEM((4, NZ, wcols, TILE), bf16),
            pltpu.VMEM((4, NX * NYL, wcols, TILE), bf16),
            pltpu.VMEM((features,), jnp.float32),
            pltpu.VMEM((features, HD), jnp.float32),
            pltpu.SMEM(tile_map.shape, jnp.int32),
            pltpu.SMEM(key_tiles.shape[::-1], jnp.int32),
            pltpu.SMEM(key_count.shape, jnp.int32),
            pltpu.SemaphoreType.DMA((8,)),
            pltpu.SemaphoreType.DMA((128,)),
            pltpu.SemaphoreType.DMA((128,)),
        ],
        compiler_params=pltpu.CompilerParams(
            collective_id=0, has_side_effects=True, vmem_limit_bytes=56 * 2**20
        ),
        cost_estimate=pl.CostEstimate(
            flops=1_100_000_000, bytes_accessed=2_000_000, transcendentals=500_000
        ),
        name="attend_project",
    )(q_heads, k_heads, v_heads, out_weight.T, out_gate, tile_map, key_tiles.T, key_count)


def solution(mesh):
    return jax.shard_map(
        on_device,
        mesh=mesh,
        in_specs=(
            P("seq", "fsdp"),
            P("seq", "fsdp"),
            P("seq", "fsdp"),
            P("fsdp", "seq"),
            P("fsdp"),
            P(),
            P(),
            P(),
        ),
        out_specs=P("fsdp", "seq"),
        check_vma=False,
    )
```

time: 83 us -> 71.5 us (0.86); the launches traced: 81.9 us -> 71.4 us
  Pallas kernels: 76.2 us -> 69.8 us
  local copies, waits for them, and re-layouts: 5.68 us -> 1.59 us
    pallas_call x1, Pallas kernels: 76.2 us -> 69.8 us  [on_device(): pl.pallas_call(kernel, out_shape=jax.ShapeDtypeStruct((features, tokens),...]
    unnamed x16 -> x1, local copies, waits for them, and re-layouts: 4.98 us -> 1.59 us
where the time goes in v2:
time: 71.5 us; the launch traced here: 71.4 us
  Pallas kernels  69.8 us (98%)
  local copies, waits for them, and re-layouts  1.59 us (2%)
    pallas_call x1, Pallas kernels, on_device(): pl.pallas_call(kernel, out_shape=jax.ShapeDtypeStruct((features, tokens),...  69.8 us
    unnamed x1, local copies, waits for them, and re-layouts  1.59 us

profile of v2, /device:TPU:1, one launch (start us, length us, event | category | flops | bytes accessed | tf_op | source)
XLA Modules:
  0.0 71.4 jit_solution(9998641485993062469)
XLA Ops:
  0.0 69.8 %attend_project.1 = bf16[640,128]{1,0:T(8,128)(2,1)} custom-call(bf16[128,640]{1,0:T(8,128)(2,1)} %q_ref.1, bf16[128,640]{1,0:T(8,128)(2,1)} %k_ref.1, bf16[128,640]{1,0:T(8,128)(2,1)} %v_ref.1, bf16[80,640]{1,0:T(8,128)(2,1)} %bitcast.2, f32[640]{0:T(1024)} %gate_ref.1, s32[64]{0:T(128)} %map_ref.1, s32[4,64]{1,0:T(4,128)} %bitcast.3, s32[64]{0:T(128)} %count_ref.1), custom_call_target="tpu_custom_call" | custom-call | flops 1100000000 | bytes 2000000 | tf_op jit(solution)/shard_map/attend_project/pallas_call | solution.py:382
  69.8 1.6 %copy.10 = bf16[640,128]{1,0:T(8,128)(2,1)} copy(bf16[640,128]{1,0:T(8,128)(2,1)} %attend_project.1) | data formatting | bytes 327680

commit v3 on v2

--- a/solution.py
+++ b/solution.py
@@ -25,7 +25,7 @@
 def kernel(
     q_ref, k_ref, v_ref, w_ref, gate_ref, map_ref, list_ref, count_ref, out_ref,
     qbuf, kv, wtmp, wall, attn, toks, keep, give, take, sbuf, rbuf, gline, gcol,
-    tile_map, key_list, key_count, local_sems, send_sems, recv_sems,
+    tile_map, key_list, key_count, obuf, out_sems, local_sems, send_sems, recv_sems,
 ):
     heads = q_ref.shape[1] // HD
     wcols = w_ref.shape[0]
@@ -84,6 +84,7 @@
     pl.semaphore_wait(barrier, len(peers))
 
     started = []
+    written = []
     table = {}
 
     def number(key):
@@ -310,7 +311,13 @@
                 for source in sources:
                     summed = summed + rbuf[piece, source, span].astype(jnp.float32)
                 gate = gcol[pl.ds(first, size), :]
-                out_ref[pl.ds(first, size), :] = (gate * summed).astype(out_ref.dtype)
+                obuf[pl.ds(first, size), :] = (gate * summed).astype(obuf.dtype)
+                out = pltpu.make_async_copy(
+                    obuf.at[pl.ds(first, size)], out_ref.at[pl.ds(first, size)],
+                    out_sems.at[(piece * 2 + part_half) * 2 + column_core],
+                )
+                out.start()
+                written.append(out)
 
     swap()
     weights_out(1)
@@ -319,6 +326,7 @@
     sibling_out()
     gate_column()
     bias = key_bias()
+    receive(("s",), kv.at[1])
     ring_step(0, 2)
     halo(0)
     weights_in(1)
@@ -333,16 +341,15 @@
     ring_step(1, 3)
     ring_step(2, 2)
     ring_step(1, 4)
+    forward(0)
     weights_in(3)
     ring_step(3, 1)
-    forward(0)
+    attention(0, bias)
     ring_step(2, 3)
-    receive(("s",), kv.at[1])
-    attention(0, bias)
+    forward(1)
     ring_step(3, 2)
-    forward(1)
+    attention(1, bias)
     ring_step(2, 4)
-    attention(1, bias)
     ring_step(3, 3)
     ring_last(0)
     tokens_in(0)
@@ -371,19 +378,20 @@
     tokens_end(1)
     for copy in started:
         copy.wait_send()
+    for copy in written:
+        copy.wait()
 
 
 def on_device(q_heads, k_heads, v_heads, out_weight, out_gate, tile_map, key_tiles, key_count):
     tokens, width = q_heads.shape
     wcols = out_weight.shape[1]
     features = out_gate.shape[0]
-    vmem = pl.BlockSpec(memory_space=pltpu.VMEM)
     bf16 = jnp.bfloat16
     return pl.pallas_call(
         kernel,
         out_shape=jax.ShapeDtypeStruct((features, tokens), bf16),
         in_specs=[pl.BlockSpec(memory_space=pl.ANY)] * 8,
-        out_specs=vmem,
+        out_specs=pl.BlockSpec(memory_space=pl.ANY),
         scratch_shapes=[
             pltpu.VMEM((TILE, width), bf16),
             pltpu.VMEM((6, 2, TILE, width), bf16),
@@ -401,6 +409,8 @@
             pltpu.SMEM(tile_map.shape, jnp.int32),
             pltpu.SMEM(key_tiles.shape[::-1], jnp.int32),
             pltpu.SMEM(key_count.shape, jnp.int32),
+            pltpu.VMEM((features, tokens), bf16),
+            pltpu.SemaphoreType.DMA((16,)),
             pltpu.SemaphoreType.DMA((8,)),
             pltpu.SemaphoreType.DMA((128,)),
             pltpu.SemaphoreType.DMA((128,)),

time: 71.5 us -> 70.4 us (0.985)
  Pallas kernels: 69.8 us -> 68.7 us
    pallas_call x1, Pallas kernels: 69.8 us -> 68.7 us  [on_device(): pl.pallas_call(kernel, out_shape=jax.ShapeDtypeStruct((features, tokens),...]
where the time goes in v3:
time: 70.4 us; the launch traced here: 70.3 us
  Pallas kernels  68.7 us (98%)
  local copies, waits for them, and re-layouts  1.59 us (2%)
    pallas_call x1, Pallas kernels, on_device(): pl.pallas_call(kernel, out_shape=jax.ShapeDtypeStruct((features, tokens),...  68.7 us
    unnamed x1, local copies, waits for them, and re-layouts  1.59 us

profile of v3, /device:TPU:1, one launch (start us, length us, event | category | flops | bytes accessed | tf_op | source)
XLA Modules:
  0.0 70.3 jit_solution(2132210074457225024)
XLA Ops:
  0.0 68.7 %attend_project.1 = bf16[640,128]{1,0:T(8,128)(2,1)} custom-call(bf16[128,640]{1,0:T(8,128)(2,1)} %q_ref.1, bf16[128,640]{1,0:T(8,128)(2,1)} %k_ref.1, bf16[128,640]{1,0:T(8,128)(2,1)} %v_ref.1, bf16[80,640]{1,0:T(8,128)(2,1)} %bitcast.2, f32[640]{0:T(1024)} %gate_ref.1, s32[64]{0:T(128)} %map_ref.1, s32[4,64]{1,0:T(4,128)} %bitcast.3, s32[64]{0:T(128)} %count_ref.1), custom_call_target="tpu_custom_call" | custom-call | flops 1100000000 | bytes 2000000 | tf_op jit(solution)/shard_map/attend_project/pallas_call | solution.py:390
  68.7 1.6 %copy.10 = bf16[640,128]{1,0:T(8,128)(2,1)} copy(bf16[640,128]{1,0:T(8,128)(2,1)} %attend_project.1) | data formatting | bytes 327680

commit v4 on v3

--- a/solution.py
+++ b/solution.py
@@ -362,15 +362,15 @@
     scatter(1)
     ring_last(2)
     project(2)
-    finish(0)
     scatter(2)
     ring_last(3, (0,))
     project(3, 0)
     ring_last(3, (1,))
     project(3, 1)
-    finish(1)
+    finish(0)
     scatter(3, 0)
     scatter(3, 1)
+    finish(1)
     finish(2)
     finish(3, 0)
     finish(3, 1)

time: 70.4 us -> 69.8 us (level)
  no operation moved by 1% of the time
where the time goes in v4:
time: 69.8 us; the launch traced here: 69.6 us
  Pallas kernels  68 us (97%)
  local copies, waits for them, and re-layouts  1.59 us (2%)
    pallas_call x1, Pallas kernels, on_device(): pl.pallas_call(kernel, out_shape=jax.ShapeDtypeStruct((features, tokens),...  68 us
    unnamed x1, local copies, waits for them, and re-layouts  1.59 us

profile of v4, /device:TPU:1, one launch (start us, length us, event | category | flops | bytes accessed | tf_op | source)
XLA Modules:
  0.0 69.6 jit_solution(13204137428499229966)
XLA Ops:
  0.0 68.0 %attend_project.1 = bf16[640,128]{1,0:T(8,128)(2,1)} custom-call(bf16[128,640]{1,0:T(8,128)(2,1)} %q_ref.1, bf16[128,640]{1,0:T(8,128)(2,1)} %k_ref.1, bf16[128,640]{1,0:T(8,128)(2,1)} %v_ref.1, bf16[80,640]{1,0:T(8,128)(2,1)} %bitcast.2, f32[640]{0:T(1024)} %gate_ref.1, s32[64]{0:T(128)} %map_ref.1, s32[4,64]{1,0:T(4,128)} %bitcast.3, s32[64]{0:T(128)} %count_ref.1), custom_call_target="tpu_custom_call" | custom-call | flops 1100000000 | bytes 2000000 | tf_op jit(solution)/shard_map/attend_project/pallas_call | solution.py:390
  68.0 1.6 %copy.10 = bf16[640,128]{1,0:T(8,128)(2,1)} copy(bf16[640,128]{1,0:T(8,128)(2,1)} %attend_project.1) | data formatting | bytes 327680

commit v5 on v4

--- a/solution.py
+++ b/solution.py
@@ -363,17 +363,13 @@
     ring_last(2)
     project(2)
     scatter(2)
-    ring_last(3, (0,))
-    project(3, 0)
-    ring_last(3, (1,))
-    project(3, 1)
+    ring_last(3)
+    project(3)
     finish(0)
-    scatter(3, 0)
-    scatter(3, 1)
+    scatter(3)
     finish(1)
     finish(2)
-    finish(3, 0)
-    finish(3, 1)
+    finish(3)
     tokens_end(0)
     tokens_end(1)
     for copy in started:

time: 69.8 us -> 70 us (level)
  no operation moved by 1% of the time
where the time goes in v5:
time: 70 us; the launch traced here: 69.9 us
  Pallas kernels  68.3 us (98%)
  local copies, waits for them, and re-layouts  1.59 us (2%)
    pallas_call x1, Pallas kernels, on_device(): pl.pallas_call(kernel, out_shape=jax.ShapeDtypeStruct((features, tokens),...  68.3 us
    unnamed x1, local copies, waits for them, and re-layouts  1.59 us

profile of v5, /device:TPU:1, one launch (start us, length us, event | category | flops | bytes accessed | tf_op | source)
XLA Modules:
  0.0 69.9 jit_solution(3847544103189305685)
XLA Ops:
  0.0 68.3 %attend_project.1 = bf16[640,128]{1,0:T(8,128)(2,1)} custom-call(bf16[128,640]{1,0:T(8,128)(2,1)} %q_ref.1, bf16[128,640]{1,0:T(8,128)(2,1)} %k_ref.1, bf16[128,640]{1,0:T(8,128)(2,1)} %v_ref.1, bf16[80,640]{1,0:T(8,128)(2,1)} %bitcast.2, f32[640]{0:T(1024)} %gate_ref.1, s32[64]{0:T(128)} %map_ref.1, s32[4,64]{1,0:T(4,128)} %bitcast.3, s32[64]{0:T(128)} %count_ref.1), custom_call_target="tpu_custom_call" | custom-call | flops 1100000000 | bytes 2000000 | tf_op jit(solution)/shard_map/attend_project/pallas_call | solution.py:386
  68.3 1.6 %copy.10 = bf16[640,128]{1,0:T(8,128)(2,1)} copy(bf16[640,128]{1,0:T(8,128)(2,1)} %attend_project.1) | data formatting | bytes 327680
